TPU v7x, 256 devices: a whole 4x4x8 slice. The times are simulated.
256 devices in a mesh: bin: 4 (over x_lo, core), row: 64 (over z, x_hi, y).
Axes of the slice: x: 4 (x_hi: 2, x_lo: 2; x = x_hi * 2 + x_lo), y: 4, z: 8, core: 2. Of those that a mesh axis runs over, the one named last changes fastest.
Arguments:
- focusing: bfloat16 [12, 2, 4096, 4096], P('bin', None, 'row'), may hold values from -0.0625 to 0.0625
- snapshots: bfloat16 [12, 2, 4096, 128], P('bin', None, 'row'), may hold values from -6 to 6
Outputs:
- spectrum: float32 [2, 4096, 4096], P(None, 'row', 'bin')
All inputs are finite; a program needn't handle non-finite values.
Results may differ from a plain program's by a relative error of at most 0.0034.
Values may be sent and summed in bfloat16 or wider, within the bound.
A program may use at most 64 MiB of HBM per device.

v0:
```python
import jax
import jax.numpy as jnp
from jax import lax
from jax.sharding import PartitionSpec as P


def contract(left, right):
    return lax.dot_general(
        left, right, (((1,), (1,)), ((), ())), preferred_element_type=jnp.float32
    )


def on_device(focusing, snapshots):
    local_bins = focusing.shape[0]
    own_rows = focusing.shape[2]
    width = focusing.shape[3]
    count = snapshots.shape[3]
    scale = 1.0 / (local_bins * lax.axis_size("bin") * count)
    pieces = []
    for index in range(local_bins):
        matrix = focusing[index]
        piece = lax.all_gather(snapshots[index], "row", axis=1, tiled=True)
        new_real = jnp.dot(matrix[0], piece[0], preferred_element_type=jnp.float32) - jnp.dot(
            matrix[1], piece[1], preferred_element_type=jnp.float32
        )
        new_imag = jnp.dot(matrix[0], piece[1], preferred_element_type=jnp.float32) + jnp.dot(
            matrix[1], piece[0], preferred_element_type=jnp.float32
        )
        pieces.append(jnp.stack([new_real, new_imag]).astype(jnp.bfloat16))
    focused = jnp.stack(pieces)
    total = jnp.zeros((2, own_rows, width), jnp.float32)
    for index in range(local_bins):
        current = focused[index]
        gram_piece = lax.all_gather(current, "row", axis=1, tiled=True)
        real_part = contract(current[0], gram_piece[0]) + contract(current[1], gram_piece[1])
        imag_part = contract(current[1], gram_piece[0]) - contract(current[0], gram_piece[1])
        total = total + jnp.stack([real_part, imag_part])
    return lax.psum_scatter(total * scale, "bin", scatter_dimension=2, tiled=True)


def solution(mesh):
    placed = (P("bin", None, "row", None), P("bin", None, "row", None))
    return jax.shard_map(
        on_device, mesh=mesh, in_specs=placed, out_specs=P(None, "row", "bin"), check_vma=False
    )
```

profile of v0, /device:TPU:1, one launch (start us, length us, event | category | flops | bytes accessed | tf_op | source)
XLA Modules:
  0.0 767.7 jit_solution(13210433172321638339)
XLA Ops:
  6.5 1.6 fusion.50
  8.1 0.0 all-gather.20.cloned.1.call-start
  8.2 0.7 all-gather.20.cloned.1.call-update
  8.9 0.0 all-gather.16.cloned.1.call-start
  8.9 0.7 all-gather.16.cloned.1.call-update
  9.6 0.0 all-gather.12.cloned.1.call-start
  9.7 119.6 %all-gather.18.cloned.1.call-done = bf16[1,2,4096,128]{3,2,1,0:T(8,128)(2,1)} async-done(((bf16[1,2,64,128]{3,2,1,0:T(8,128)(2,1)}), bf16[1,2,4096,128]{3,2,1,0:T(8,128)(2,1)}) %all-gather.18.cloned.1.call-update) | async-done | bytes 2097168 | tf_op jit(solution)/shard_map/all_gather | solution.py:22
  129.2 1.7 fusion.18
  131.0 1.8 fusion.19
  132.8 1.5 fusion.10
  134.4 0.3 fusion.11
  134.7 0.6 pad_maximum_fusion.1
  135.3 0.0 all-gather.14.cloned.1.call-start
  135.4 112.2 %all-gather.20.cloned.1.call-done = bf16[1,2,4096,128]{3,2,1,0:T(8,128)(2,1)} async-done(((bf16[1,2,64,128]{3,2,1,0:T(8,128)(2,1)}), bf16[1,2,4096,128]{3,2,1,0:T(8,128)(2,1)}) %all-gather.20.cloned.1.call-update) | async-done | bytes 2097168 | tf_op jit(solution)/shard_map/all_gather | solution.py:22
  247.5 1.7 fusion.22
  249.2 1.5 fusion.23
  250.8 0.3 fusion.12
  251.1 0.3 fusion.13
  251.4 0.6 pad_maximum_fusion.2
  252.1 0.0 all-gather.10.cloned.1.call-start
  252.1 113.7 %all-gather.16.cloned.1.call-done = bf16[1,2,4096,128]{3,2,1,0:T(8,128)(2,1)} async-done(((bf16[1,2,64,128]{3,2,1,0:T(8,128)(2,1)}), bf16[1,2,4096,128]{3,2,1,0:T(8,128)(2,1)}) %all-gather.16.cloned.1.call-update) | async-done | bytes 2097168 | tf_op jit(solution)/shard_map/all_gather | solution.py:22
  365.9 1.7 fusion.14
  367.5 1.5 fusion.15
  369.1 0.3 fusion.8
  369.4 0.3 fusion.9
  369.7 0.6 pad_maximum_fusion
  370.4 0.0 reduce-scatter.2.cloned.1.call-start
  370.4 113.6 %all-gather.12.cloned.1.call-done = bf16[2,4096,128]{2,1,0:T(8,128)(2,1)} async-done(((bf16[2,64,128]{2,1,0:T(8,128)(2,1)}), bf16[2,4096,128]{2,1,0:T(8,128)(2,1)}) %all-gather.12.cloned.1.call-update) | async-done | bytes 2097168 | tf_op jit(solution)/shard_map/all_gather | solution.py:34
  484.0 2.8 fusion.21
  486.8 1.5 fusion.20
  488.3 113.9 %all-gather.14.cloned.1.call-done = bf16[2,4096,128]{2,1,0:T(8,128)(2,1)} async-done(((bf16[2,64,128]{2,1,0:T(8,128)(2,1)}), bf16[2,4096,128]{2,1,0:T(8,128)(2,1)}) %all-gather.14.cloned.1.call-update) | async-done | bytes 2097168 | tf_op jit(solution)/shard_map/all_gather | solution.py:34
  602.2 2.8 fusion.25
  605.0 0.5 fusion.24
  605.5 114.8 %all-gather.10.cloned.1.call-done = bf16[2,4096,128]{2,1,0:T(8,128)(2,1)} async-done(((bf16[2,64,128]{2,1,0:T(8,128)(2,1)}), bf16[2,4096,128]{2,1,0:T(8,128)(2,1)}) %all-gather.10.cloned.1.call-update) | async-done | bytes 2097168 | tf_op jit(solution)/shard_map/all_gather | solution.py:34
  720.3 1.8 fusion.17
  722.2 0.1 copy-done.3
  722.2 0.5 fusion.16
  722.7 0.5 fusion.2
  723.2 0.7 copy-done.4
  723.9 0.5 fusion.3
  724.4 1.1 copy-done.2
  725.5 0.3 copy-done.5
  725.8 0.5 fusion.4
  726.3 0.5 fusion.5
  726.8 0.5 fusion
  727.3 0.5 fusion.1
  727.7 1.7 fusion.7
  729.5 31.4 %reduce-scatter.2.cloned.1.call-done = f32[2,64,1024]{2,1,0:T(8,128)} async-done(((f32[2,64,4096]{2,1,0:T(8,128)}), f32[2,64,1024]{2,1,0:T(8,128)}) %reduce-scatter.2.cloned.1.call-update) | async-done | bytes 524304 | tf_op jit(solution)/shard_map/reduce_scatter | solution.py:38
  (24 shorter events, 0.1 us)
Async XLA Ops:
  6.5 126.3 %copy-start.7 = (bf16[3,2,64,4096]{3,2,1,0:T(8,128)(2,1)S(1)}, bf16[3,2,64,4096]{3,2,1,0:T(8,128)(2,1)}, u32[]{:S(2)}) copy-start(bf16[3,2,64,4096]{3,2,1,0:T(8,128)(2,1)} %param.2) | copy-start | bytes 9437188
  6.5 122.7 %all-gather.18.cloned.1.call-start = ((), (), s32[]{:S(2)}) async-start(), calls=%async_computation.6 | async-start | bytes 2129920 | tf_op jit(solution)/shard_map/all_gather | solution.py:22
  8.1 239.4 %all-gather.20.cloned.1.call-start = ((), (), s32[]{:S(2)}) async-start(), calls=%async_computation.7 | async-start | bytes 2129920 | tf_op jit(solution)/shard_map/all_gather | solution.py:22
  8.9 357.0 %all-gather.16.cloned.1.call-start = ((), (), s32[]{:S(2)}) async-start(), calls=%async_computation.5 | async-start | bytes 2129920 | tf_op jit(solution)/shard_map/all_gather | solution.py:22
  9.6 474.4 %all-gather.12.cloned.1.call-start = ((), (), s32[]{:S(2)}) async-start(), calls=%async_computation.2 | async-start | bytes 2129920 | tf_op jit(solution)/shard_map/all_gather | solution.py:34
  130.9 3.4 copy-start.10
  135.3 466.8 %all-gather.14.cloned.1.call-start = ((), (), s32[]{:S(2)}) async-start(), calls=%async_computation.3 | async-start | bytes 2129920 | tf_op jit(solution)/shard_map/all_gather | solution.py:34
  247.5 3.2 copy-start.9
  252.1 468.2 %all-gather.10.cloned.1.call-start = ((), (), s32[]{:S(2)}) async-start(), calls=%async_computation.1 | async-start | bytes 2129920 | tf_op jit(solution)/shard_map/all_gather | solution.py:34
  365.9 3.2 copy-start.8
  370.4 390.5 %reduce-scatter.2.cloned.1.call-start = ((), (), s32[]{:S(2)}) async-start(), calls=%async_computation.4 | async-start | bytes 2621440 | tf_op jit(solution)/shard_map/reduce_scatter | solution.py:38
  484.0 2.8 copy-start
  602.2 2.8 copy-start.1
  720.3 1.9 copy-start.3
  720.3 2.4 copy-start.6
  722.7 1.2 copy-start.4
  723.9 1.6 copy-start.2
  723.9 1.9 copy-start.5
Sparse Core Ops, SparseCore 0:
  10.9 118.3 all-gather.17
  132.7 114.7 all-gather.19
  251.1 114.7 all-gather.15
  369.2 114.7 all-gather.11
  487.4 114.7 all-gather.13
  605.5 114.7 all-gather.9
  729.6 31.2 reduce-scatter.1
where the time goes:
time: 768 us
  waiting for transfers between devices  721 us (94%)
  matrix products  25.9 us (3%)
  between operations  13.7 us (2%)
    all_gather x3, waiting for transfers between devices, on_device(): piece = lax.all_gather(snapshots[index], 'row', axis=1, tiled=True)  345 us
    all_gather x3, waiting for transfers between devices, on_device(): gram_piece = lax.all_gather(current, 'row', axis=1, tiled=True)  342 us
    reduce_scatter x1, waiting for transfers between devices, on_device(): lax.psum_scatter(total * scale, 'bin', scatter_dimension=2, tiled=True)  31.4 us
  transfers between devices with their start and end apart: 7, of which 7 were waited for; matrix products, arithmetic and copies ran while one was open for 3% of the time, Pallas kernels for 0%

commit v1 on v0

v1 whole, which is shorter than its diff:
```python
import functools

import jax
import jax.numpy as jnp
from jax import lax
from jax.experimental import pallas as pl
from jax.experimental.pallas import tpu as pltpu
from jax.sharding import PartitionSpec as P

MESH = pl.DeviceIdType.MESH
BF16 = jnp.bfloat16
F32 = jnp.float32

SPLIT = (
    {"X": (0, 32), "Y": (32, 16), "Z": (48, 16)},
    {"X": (0, 16), "Y": (16, 32), "Z": (48, 16)},
    {"X": (0, 16), "Y": (16, 16), "Z": (32, 32)},
)
GAP = 3
N_COPIES = 256


def dot_t(left, right):
    return lax.dot_general(left, right, (((1,), (1,)), ((), ())), preferred_element_type=F32)


def kernel(scale, foc, snap, out, T, X, yrow, ycol, G, gin, S, R, tsem, ssem, rsem):
    b = lax.axis_index("bin")
    row = lax.axis_index("row")
    xl, c = b // 2, b % 2
    z, xh, y = row // 8, (row // 4) % 2, row % 4

    def at(dz=0, dx=0, dy=0):
        return (b, ((z + dz) % 8) * 8 + ((xh + dx) % 2) * 4 + (y + dy) % 4)

    loads = [pltpu.make_async_copy(foc.at[k], T.at[k], tsem.at[k]) for k in range(3)]
    for k in range(3):
        loads[k].start()

    partners = [at(dz=d) for d in range(1, 8)]
    for dl in range(2):
        for dx in range(2):
            for dy in range(4):
                if dl or dx or dy:
                    partners.append((((xl + dl) % 2) * 2 + c, z * 8 + ((xh + dx) % 2) * 4 + (y + dy) % 4))
    sibling = (xl * 2 + 1 - c, row)
    partners.append(sibling)
    barrier = pltpu.get_barrier_semaphore()
    for peer in partners:
        pl.semaphore_signal(barrier, inc=1, device_id=peer, device_id_type=MESH)

    for k in range(3):
        X[k, z, xh, y] = jnp.concatenate([snap[k, 0], snap[k, 1]], axis=1)

    pl.semaphore_wait(barrier, len(partners))

    count = [0]
    sent = []

    def send(src, dst, landing, peer):
        i = count[0]
        count[0] += 1
        copy = pltpu.make_async_remote_copy(
            src_ref=src, dst_ref=dst, send_sem=ssem.at[i], recv_sem=rsem.at[i], device_id=peer, device_id_type=MESH
        )
        copy.start()
        sent.append(copy)
        arrival = pltpu.make_async_remote_copy(
            src_ref=landing, dst_ref=landing, send_sem=ssem.at[i], recv_sem=rsem.at[i], device_id=peer, device_id_type=MESH
        )
        return arrival.wait_recv

    def wait_all(waits):
        for w in waits:
            w()

    def bin_steps(k):
        rx, ry, rz = (pl.ds(*SPLIT[k][t]) for t in "XYZ")
        w = {}

        def zfirst(name, rs):
            own = X.at[k, z, xh, y, rs]
            w[name] = [send(own, own, X.at[k, (z + 8 - d) % 8, xh, y, rs], at(dz=d)) for d in (4, 3, 5, 2, 6, 1, 7)]

        def s0():
            own = X.at[k, z, xh, y, rz]
            w["Z1"] = [send(own, own, X.at[k, z, 1 - xh, y, rz], at(dx=1))]
            zfirst("X1", rx)
            zfirst("Y1", ry)

        def s1():
            wait_all(w["Z1"])
            own = X.at[k, z, :, y, rz]
            w["Z2"] = [send(own, own, X.at[k, z, :, (y + 4 - d) % 4, rz], at(dy=d)) for d in (2, 1, 3)]
            wait_all(w["X1"])
            own = X.at[k, :, xh, y, rx]
            w["X2"] = [send(own, own, X.at[k, :, xh, (y + 4 - d) % 4, rx], at(dy=d)) for d in (2, 1, 3)]
            wait_all(w["Y1"])
            own = X.at[k, :, xh, y, ry]
            w["Y2"] = [send(own, own, X.at[k, :, 1 - xh, y, ry], at(dx=1))]

        def zring(far, halves_up, halves_down):
            up = [None, None]
            down = [None, None]
            for h in halves_up:
                piece = X.at[k, (z + 8 - far) % 8, h, :, rz]
                up[h] = send(piece, piece, X.at[k, (z + 8 - far - 1) % 8, h, :, rz], at(dz=1))
            for h in halves_down:
                piece = X.at[k, (z + far) % 8, h, :, rz]
                down[h] = send(piece, piece, X.at[k, (z + far + 1) % 8, h, :, rz], at(dz=7))
            return up, down

        def forward(far):
            up0, down0 = w["ring"]
            up, down = [None, None], [None, None]
            for h in range(2):
                up0[h]()
                if far < 3 or h == 0:
                    piece = X.at[k, (z + 8 - far) % 8, h, :, rz]
                    up[h] = send(piece, piece, X.at[k, (z + 8 - far - 1) % 8, h, :, rz], at(dz=1))
                down0[h]()
                if far < 3 or h == 1:
                    piece = X.at[k, (z + far) % 8, h, :, rz]
                    down[h] = send(piece, piece, X.at[k, (z + far + 1) % 8, h, :, rz], at(dz=7))
            w["ring"] = up, down

        def s2():
            wait_all(w["Z2"])
            w["ring"] = zring(0, (0, 1), (0, 1))
            wait_all(w["Y2"])
            own = X.at[k, :, :, y, ry]
            w["Y3"] = [send(own, own, X.at[k, :, :, (y + 4 - d) % 4, ry], at(dy=d)) for d in (1, 3)]
            wait_all(w["X2"])
            own = X.at[k, :, xh, :, rx]
            w["X3"] = [send(own, own, X.at[k, :, 1 - xh, :, rx], at(dx=1))]

        def s3():
            forward(1)
            w["Y3"][0]()
            piece = X.at[k, :, 0, (y + 3) % 4, ry]
            up = send(piece, piece, X.at[k, :, 0, (y + 2) % 4, ry], at(dy=1))
            w["Y3"][1]()
            piece = X.at[k, :, 1, (y + 1) % 4, ry]
            down = send(piece, piece, X.at[k, :, 1, (y + 2) % 4, ry], at(dy=3))
            w["Y4"] = [up, down]

        def s4():
            forward(2)

        def s5():
            forward(3)

        def s6():
            up, down = w["ring"]
            up[0]()
            down[1]()
            wait_all(w["Y4"])
            wait_all(w["X3"])
            loads[k].wait()

            def plane(i, acc):
                cols = pl.ds(pl.multiple_of(i * 512, 512), 512)
                return acc + jnp.dot(
                    T[k, :, :, cols].reshape(128, 512), X[k, i].reshape(512, 256), preferred_element_type=F32
                )

            acc = lax.fori_loop(0, 8, plane, jnp.zeros((128, 256), F32))
            real = acc[:64, :128] - acc[64:, 128:]
            imag = acc[:64, 128:] + acc[64:, :128]
            focused = jnp.concatenate([real, imag], axis=1).astype(BF16)
            yrow[k, xh, y] = focused
            ycol[k, z] = focused
            own = ycol.at[k, z]
            w["C"] = [send(own, own, ycol.at[k, (z + 8 - d) % 8], at(dz=d)) for d in (4, 3, 5, 2, 6, 1, 7)]
            own = yrow.at[k, xh, y]
            w["R"] = [
                send(own, own, yrow.at[k, (xh + dx) % 2, (y + 4 - dy) % 4], at(dx=dx, dy=dy))
                for dx, dy in ((1, 2), (1, 1), (1, 3), (1, 0), (0, 2), (0, 1), (0, 3))
            ]

        def s7():
            wait_all(w["C"])
            wait_all(w["R"])
            if k < 2:
                for part in range(2):
                    for half in range(2):
                        gram(k, part, half)

        return [s0, s1, s2, s3, s4, s5, s6, s7]

    def gram(k, part, half):
        left = yrow[k, half].reshape(256, 256)
        right = jnp.concatenate(
            [ycol[k, pl.ds(2 * part, 2)].reshape(128, 256), ycol[k, pl.ds(4 + 2 * part, 2)].reshape(128, 256)], axis=0
        )
        turned = jnp.concatenate([-right[:, 128:], right[:, :128]], axis=1)
        if k == 0:
            G[part, half, 0] = dot_t(left, right)
            G[part, half, 1] = dot_t(left, turned)
        else:
            G[part, half, 0] += dot_t(left, right)
            G[part, half, 1] += dot_t(left, turned)

    events = []
    for k in range(3):
        for i, step in enumerate(bin_steps(k)):
            events.append((k * GAP + i, -i, k, step))
    for e in sorted(events, key=lambda e: e[:3]):
        e[3]()

    waits = []
    for half in ((xh + 1) % 2, xh):
        gram(2, 1 - c, half)
        piece = G.at[1 - c, half]
        waits.append(send(piece, gin.at[half], gin.at[half], sibling))
    final = []
    for n, half in enumerate(((xh + 1) % 2, xh)):
        gram(2, c, half)
        waits[n]()
        total = (G[c, half] + gin[half]) * scale
        for part in range(2):
            S[part, half] = total[:, :, part * 128 : (part + 1) * 128].reshape(2, 4, 64, 128).astype(BF16)
        dx = 1 - n
        for dl, dy in ((1, 2), (1, 1), (1, 3), (0, 2), (0, 1), (0, 3), (1, 0), (0, 0)):
            if dl or dx or dy:
                to_l, to_x, to_y = (xl + dl) % 2, (xh + dx) % 2, (y + dy) % 4
                final.append(
                    send(
                        S.at[to_l, to_x, :, to_y],
                        R.at[xl, xh, y],
                        R.at[(xl + dl) % 2, (xh + dx) % 2, (y + 4 - dy) % 4],
                        (to_l * 2 + c, z * 8 + to_x * 4 + to_y),
                    )
                )
    R[xl, xh, y] = S[xl, xh, :, y]
    wait_all(final)
    for zi in range(2):
        for h in range(2):
            for yp in range(2):
                lanes = slice(zi * 64, zi * 64 + 64)
                pair = [
                    R[0, h, 2 * yp + o].astype(F32) + R[1, h, 2 * yp + o].astype(F32) for o in range(2)
                ]
                out[:, :, zi * 512 + h * 256 + yp * 128 : zi * 512 + h * 256 + yp * 128 + 128] = jnp.concatenate(
                    [pair[0][:, :, lanes], pair[1][:, :, lanes]], axis=2
                )
    for copy in sent:
        copy.wait_send()


def on_device(focusing, snapshots):
    scale = 1.0 / (12 * 128)
    return pl.pallas_call(
        functools.partial(kernel, scale),
        out_shape=jax.ShapeDtypeStruct((2, 64, 1024), F32),
        in_specs=[pl.BlockSpec(memory_space=pl.ANY), pl.BlockSpec(memory_space=pltpu.VMEM)],
        out_specs=pl.BlockSpec(memory_space=pltpu.VMEM),
        scratch_shapes=[
            pltpu.VMEM((3, 2, 64, 4096), BF16),
            pltpu.VMEM((3, 8, 2, 4, 64, 256), BF16),
            pltpu.VMEM((3, 2, 4, 64, 256), BF16),
            pltpu.VMEM((3, 8, 64, 256), BF16),
            pltpu.VMEM((2, 2, 2, 256, 256), F32),
            pltpu.VMEM((2, 2, 256, 256), F32),
            pltpu.VMEM((2, 2, 2, 4, 64, 128), BF16),
            pltpu.VMEM((2, 2, 4, 2, 64, 128), BF16),
            pltpu.SemaphoreType.DMA((3,)),
            pltpu.SemaphoreType.DMA((N_COPIES,)),
            pltpu.SemaphoreType.DMA((N_COPIES,)),
        ],
        compiler_params=pltpu.CompilerParams(
            collective_id=0, has_side_effects=True, vmem_limit_bytes=48 * 2**20
        ),
        name="focus_gram",
    )(focusing, snapshots)


def solution(mesh):
    placed = (P("bin", None, "row", None), P("bin", None, "row", None))
    return jax.shard_map(
        on_device, mesh=mesh, in_specs=placed, out_specs=P(None, "row", "bin"), check_vma=False
    )
```

time: 768 us -> 108 us (0.14)
  waiting for transfers between devices: 721 us -> 0 us
  Pallas kernels: 0 us -> 105 us
  matrix products: 25.9 us -> 0 us
  between operations: 13.7 us -> 0.01 us
    all_gather x6 -> x0, waiting for transfers between devices: 688 us -> none  [the longest x3 345 us: on_device(): piece = lax.all_gather(snapshots[index], 'row', axis=1, tiled=True)]
    pallas_call x0 -> x1, Pallas kernels: none -> 105 us  [on_device(): pl.pallas_call(functools.partial(kernel, scale), out_shape=jax.ShapeDtype...]
    reduce_scatter x1 -> x0, waiting for transfers between devices: 31.4 us -> none  [on_device(): lax.psum_scatter(total * scale, 'bin', scatter_dimension=2, tiled=True)]
    dot_general x24 -> x0, matrix products: 25.9 us -> none  [the longest x12 12.8 us: contract(): lax.dot_general(left, right, (((1,), (1,)), ((), ())), preferred_element_...]
  transfers between devices with their start and end apart: 7 -> 0, of which waited for: 7 -> 0; matrix products, arithmetic and copies ran while one was open for 3% -> 0% of each run, Pallas kernels for 0% -> 0%
where the time goes in v1:
time: 108 us
  Pallas kernels  105 us (97%)
  local copies, waits for them, and re-layouts  3.58 us (3%)
    pallas_call x1, Pallas kernels, on_device(): pl.pallas_call(functools.partial(kernel, scale), out_shape=jax.ShapeDtype...  105 us
    unnamed x5, local copies, waits for them, and re-layouts  3.58 us

profile of v1, /device:TPU:1, one launch (start us, length us, event | category | flops | bytes accessed | tf_op | source)
XLA Modules:
  0.0 108.2 jit_solution(11612358099572219922)
XLA Ops:
  0.0 0.0 copy-start
  0.0 1.9 %copy-done = bf16[3,2,64,4096]{3,2,1,0:T(8,128)(2,1)S(1)} copy-done((bf16[3,2,64,4096]{3,2,1,0:T(8,128)(2,1)S(1)}, bf16[3,2,64,4096]{3,2,1,0:T(8,128)(2,1)}, u32[]{:S(2)}) %copy-start) | copy-done | bytes 3145752
  1.9 0.0 copy-start.1
  1.9 0.9 copy-done.1
  2.8 104.6 %focus_gram.1 = f32[2,64,1024]{2,1,0:T(8,128)S(1)} custom-call(bf16[3,2,64,4096]{3,2,1,0:T(8,128)(2,1)S(1)} %copy-done, bf16[3,2,64,128]{3,2,1,0:T(8,128)(2,1)S(1)} %copy-done.1), custom_call_target="tpu_custom_call" | custom-call | tf_op jit(solution)/shard_map/focus_gram/pallas_call | solution.py:253
  107.4 0.8 copy.4
Async XLA Ops:
  0.0 1.9 %copy-start = (bf16[3,2,64,4096]{3,2,1,0:T(8,128)(2,1)S(1)}, bf16[3,2,64,4096]{3,2,1,0:T(8,128)(2,1)}, u32[]{:S(2)}) copy-start(bf16[3,2,64,4096]{3,2,1,0:T(8,128)(2,1)} %foc.1) | copy-start | bytes 9437188
  1.9 0.9 copy-start.1

commit v2 on v1

v2 whole, which is shorter than its diff:
```python
import functools

import jax
import jax.numpy as jnp
from jax import lax
from jax.experimental import pallas as pl
from jax.experimental.pallas import tpu as pltpu
from jax.sharding import PartitionSpec as P

MESH = pl.DeviceIdType.MESH
BF16 = jnp.bfloat16
F32 = jnp.float32

PIECES = (
    (0, "X", 0, 32), (0, "Y", 32, 32),
    (1, "X", 0, 32), (1, "Y", 32, 32),
    (2, "Z", 0, 64),
)
ORDER = (0, 1, 2)
WHEN = {
    "X": {0: (0.2, 5, 12), 1: (0.4, 9, 18)},
    "Y": {0: (0.1, 4.5, 9, 16, 20), 1: (0.3, 8.5, 12, 19, 25)},
    "Z": {2: (0, 3, 6, 11, 16, 21)},
}
DONE = {0: 30, 1: 36, 2: 40}
GRAM = {0: 41, 1: 42, 2: 50}
N_COPIES = 256


def dot_t(left, right):
    return lax.dot_general(left, right, (((1,), (1,)), ((), ())), preferred_element_type=F32)


def kernel(scale, foc, snap_hbm, out, snap, T, X, yrow, ycol, G, gin, S, R, tsem, ssem, rsem):
    b = lax.axis_index("bin")
    row = lax.axis_index("row")
    xl, c = b // 2, b % 2
    z, xh, y = row // 8, (row // 4) % 2, row % 4

    def at(dz=0, dx=0, dy=0):
        return (b, ((z + dz) % 8) * 8 + ((xh + dx) % 2) * 4 + (y + dy) % 4)

    fetch = pltpu.make_async_copy(snap_hbm, snap, tsem.at[3])
    fetch.start()
    loads = [pltpu.make_async_copy(foc.at[k], T.at[k], tsem.at[k]) for k in range(3)]
    for k in range(3):
        loads[k].start()

    partners = [at(dz=d) for d in range(1, 8)]
    for dl in range(2):
        for dx in range(2):
            for dy in range(4):
                if dl or dx or dy:
                    partners.append((((xl + dl) % 2) * 2 + c, z * 8 + ((xh + dx) % 2) * 4 + (y + dy) % 4))
    sibling = (xl * 2 + 1 - c, row)
    partners.append(sibling)
    barrier = pltpu.get_barrier_semaphore()
    for peer in partners:
        pl.semaphore_signal(barrier, inc=1, device_id=peer, device_id_type=MESH)

    fetch.wait()
    for k in range(3):
        X[k, z, xh, y] = jnp.concatenate([snap[k, 0], snap[k, 1]], axis=1)

    pl.semaphore_wait(barrier, len(partners))

    count = [0]
    sent = []

    def send(src, dst, landing, peer):
        i = count[0]
        count[0] += 1
        copy = pltpu.make_async_remote_copy(
            src_ref=src, dst_ref=dst, send_sem=ssem.at[i], recv_sem=rsem.at[i], device_id=peer, device_id_type=MESH
        )
        copy.start()
        sent.append(copy)
        arrival = pltpu.make_async_remote_copy(
            src_ref=landing, dst_ref=landing, send_sem=ssem.at[i], recv_sem=rsem.at[i], device_id=peer, device_id_type=MESH
        )
        return arrival.wait_recv

    def wait_all(waits):
        for w in waits:
            w()

    events = []
    pending = {k: [] for k in range(3)}

    def event(when, step):
        events.append((when, len(events), step))

    def z_direct(k, rs):
        own = X.at[k, z, xh, y, rs]
        return [send(own, own, X.at[k, (z + 8 - d) % 8, xh, y, rs], at(dz=d)) for d in (4, 3, 5, 2, 6, 1, 7)]

    def order_x(k, rs, when):
        w = {}

        def to_x(dy):
            own = X.at[k, :, xh, (y + 4 - dy) % 4, rs]
            pending[k].append(send(own, own, X.at[k, :, 1 - xh, (y + 4 - dy) % 4, rs], at(dx=1)))

        def first():
            w["z"] = z_direct(k, rs)

        def second():
            wait_all(w["z"])
            own = X.at[k, :, xh, y, rs]
            w["y"] = [send(own, own, X.at[k, :, xh, (y + 4 - d) % 4, rs], at(dy=d)) for d in (1, 3, 2)]
            to_x(0)

        def third():
            for n, d in enumerate((1, 3, 2)):
                w["y"][n]()
                to_x(d)

        for t, step in zip(when, (first, second, third)):
            event(t, step)

    def order_y(k, rs, when):
        w = {}
        low, high = pl.ds(0, 4), pl.ds(4, 4)

        def to_y(h):
            own = X.at[k, :, h, y, rs]
            return [send(own, own, X.at[k, :, h, (y + 4 - d) % 4, rs], at(dy=d)) for d in (1, 3)]

        def on_y(h, arrivals):
            arrivals[0]()
            piece = X.at[k, low, h, (y + 3) % 4, rs]
            pending[k].append(send(piece, piece, X.at[k, low, h, (y + 2) % 4, rs], at(dy=1)))
            arrivals[1]()
            piece = X.at[k, high, h, (y + 1) % 4, rs]
            pending[k].append(send(piece, piece, X.at[k, high, h, (y + 2) % 4, rs], at(dy=3)))

        def first():
            w["z"] = z_direct(k, rs)

        def second():
            wait_all(w["z"])
            own = X.at[k, :, xh, y, rs]
            w["x"] = send(own, own, X.at[k, :, 1 - xh, y, rs], at(dx=1))
            w["a"] = to_y(xh)

        def third():
            w["x"]()
            w["b"] = to_y(1 - xh)

        def fourth():
            on_y(xh, w["a"])

        def fifth():
            on_y(1 - xh, w["b"])

        for t, step in zip(when, (first, second, third, fourth, fifth)):
            event(t, step)

    def order_z(k, rs, when):
        w = {}
        ring = {}

        def pass_on(far, d):
            line = (y + 4 - d) % 4
            if far < 4:
                if far:
                    ring[d][0]()
                h = pl.ds(0, 2) if far < 3 else pl.ds(0, 1)
                piece = X.at[k, (z + 8 - far) % 8, h, line, rs]
                up = send(piece, piece, X.at[k, (z + 7 - far) % 8, h, line, rs], at(dz=1))
                if far:
                    ring[d][1]()
                h = pl.ds(0, 2) if far < 3 else pl.ds(1, 1)
                piece = X.at[k, (z + far) % 8, h, line, rs]
                down = send(piece, piece, X.at[k, (z + far + 1) % 8, h, line, rs], at(dz=7))
                ring[d] = (up, down)
                if far == 3:
                    pending[k].extend((up, down))

        def first():
            own = X.at[k, z, xh, y, rs]
            w["x"] = send(own, own, X.at[k, z, 1 - xh, y, rs], at(dx=1))

        def second():
            w["x"]()
            own = X.at[k, z, :, y, rs]
            w["y"] = [send(own, own, X.at[k, z, :, (y + 4 - d) % 4, rs], at(dy=d)) for d in (1, 3, 2)]
            pass_on(0, 0)

        def third():
            for n, d in enumerate((1, 3, 2)):
                w["y"][n]()
                pass_on(0, d)

        def later(far):
            for d in (0, 1, 3, 2):
                pass_on(far, d)

        for t, step in zip(when, (first, second, third)):
            event(t, step)
        for far in range(1, 4):
            event(when[2 + far], functools.partial(later, far))

    def done(k):
        w = gathers[k] = []
        wait_all(pending[k])
        loads[k].wait()

        def plane(i, acc):
            cols = pl.ds(pl.multiple_of(i * 512, 512), 512)
            return acc + jnp.dot(
                T[k, :, :, cols].reshape(128, 512), X[k, i].reshape(512, 256), preferred_element_type=F32
            )

        acc = lax.fori_loop(0, 8, plane, jnp.zeros((128, 256), F32))
        real = acc[:64, :128] - acc[64:, 128:]
        imag = acc[:64, 128:] + acc[64:, :128]
        focused = jnp.concatenate([real, imag], axis=1).astype(BF16)
        yrow[k, xh, y] = focused
        ycol[k, z] = focused
        own = ycol.at[k, z]
        for d in (4, 3, 5, 2, 6, 1, 7):
            w.append(send(own, own, ycol.at[k, (z + 8 - d) % 8], at(dz=d)))
        own = yrow.at[k, xh, y]
        for dx, dy in ((1, 2), (1, 1), (1, 3), (1, 0), (0, 2), (0, 1), (0, 3)):
            w.append(send(own, own, yrow.at[k, (xh + dx) % 2, (y + 4 - dy) % 4], at(dx=dx, dy=dy)))

    def gathered(k):
        wait_all(gathers[k])
        if k != ORDER[2]:
            for part in range(2):
                for half in range(2):
                    gram(k, part, half)

    gathers = {}
    def gram(k, part, half):
        left = yrow[k, half].reshape(256, 256)
        right = jnp.concatenate(
            [ycol[k, pl.ds(2 * part, 2)].reshape(128, 256), ycol[k, pl.ds(4 + 2 * part, 2)].reshape(128, 256)], axis=0
        )
        turned = jnp.concatenate([-right[:, 128:], right[:, :128]], axis=1)
        if k == ORDER[0]:
            G[part, half, 0] = dot_t(left, right)
            G[part, half, 1] = dot_t(left, turned)
        else:
            G[part, half, 0] += dot_t(left, right)
            G[part, half, 1] += dot_t(left, turned)

    for k, kind, first_row, rows in PIECES:
        make = {"X": order_x, "Y": order_y, "Z": order_z}[kind]
        make(k, pl.ds(first_row, rows), WHEN[kind][k])
    for k in ORDER:
        event(DONE[k], functools.partial(done, k))
        event(GRAM[k], functools.partial(gathered, k))
    for e in sorted(events, key=lambda e: e[:2]):
        e[2]()

    waits = []
    for half in ((xh + 1) % 2, xh):
        gram(ORDER[2], 1 - c, half)
        piece = G.at[1 - c, half]
        waits.append(send(piece, gin.at[half], gin.at[half], sibling))
    final = []
    for n, half in enumerate(((xh + 1) % 2, xh)):
        gram(ORDER[2], c, half)
        waits[n]()
        total = (G[c, half] + gin[half]) * scale
        for part in range(2):
            S[part, half] = total[:, :, part * 128 : (part + 1) * 128].reshape(2, 4, 64, 128).astype(BF16)
        dx = 1 - n
        for dl, dy in ((1, 2), (1, 1), (1, 3), (0, 2), (0, 1), (0, 3), (1, 0), (0, 0)):
            if dl or dx or dy:
                to_l, to_x, to_y = (xl + dl) % 2, (xh + dx) % 2, (y + dy) % 4
                final.append(
                    send(
                        S.at[to_l, to_x, :, to_y],
                        R.at[xl, xh, y],
                        R.at[(xl + dl) % 2, (xh + dx) % 2, (y + 4 - dy) % 4],
                        (to_l * 2 + c, z * 8 + to_x * 4 + to_y),
                    )
                )
    R[xl, xh, y] = S[xl, xh, :, y]
    wait_all(final)
    for zi in range(2):
        for h in range(2):
            for yp in range(2):
                lanes = slice(zi * 64, zi * 64 + 64)
                pair = [
                    R[0, h, 2 * yp + o].astype(F32) + R[1, h, 2 * yp + o].astype(F32) for o in range(2)
                ]
                out[:, :, zi * 512 + h * 256 + yp * 128 : zi * 512 + h * 256 + yp * 128 + 128] = jnp.concatenate(
                    [pair[0][:, :, lanes], pair[1][:, :, lanes]], axis=2
                )
    for copy in sent:
        copy.wait_send()


def on_device(focusing, snapshots):
    scale = 1.0 / (12 * 128)
    return pl.pallas_call(
        functools.partial(kernel, scale),
        out_shape=jax.ShapeDtypeStruct((2, 64, 1024), F32),
        in_specs=[pl.BlockSpec(memory_space=pl.ANY)] * 2,
        out_specs=pl.BlockSpec(memory_space=pltpu.VMEM),
        scratch_shapes=[
            pltpu.VMEM((3, 2, 64, 128), BF16),
            pltpu.VMEM((3, 2, 64, 4096), BF16),
            pltpu.VMEM((3, 8, 2, 4, 64, 256), BF16),
            pltpu.VMEM((3, 2, 4, 64, 256), BF16),
            pltpu.VMEM((3, 8, 64, 256), BF16),
            pltpu.VMEM((2, 2, 2, 256, 256), F32),
            pltpu.VMEM((2, 2, 256, 256), F32),
            pltpu.VMEM((2, 2, 2, 4, 64, 128), BF16),
            pltpu.VMEM((2, 2, 4, 2, 64, 128), BF16),
            pltpu.SemaphoreType.DMA((4,)),
            pltpu.SemaphoreType.DMA((N_COPIES,)),
            pltpu.SemaphoreType.DMA((N_COPIES,)),
        ],
        compiler_params=pltpu.CompilerParams(
            collective_id=0, has_side_effects=True, vmem_limit_bytes=63 * 2**20
        ),
        name="focus_gram",
    )(focusing, snapshots)


def solution(mesh):
    placed = (P("bin", None, "row", None), P("bin", None, "row", None))
    return jax.shard_map(
        on_device, mesh=mesh, in_specs=placed, out_specs=P(None, "row", "bin"), check_vma=False
    )
```

time: 108 us -> 82.8 us (0.77)
  Pallas kernels: 105 us -> 80.8 us
  local copies, waits for them, and re-layouts: 3.58 us -> 1.89 us
    pallas_call x1, Pallas kernels: 105 us -> 80.8 us  [on_device(): pl.pallas_call(functools.partial(kernel, scale), out_shape=jax.ShapeDtype...]
    unnamed x5 -> x1, local copies, waits for them, and re-layouts: 3.58 us -> 1.89 us
where the time goes in v2:
time: 82.8 us; the launch traced here: 82.6 us
  Pallas kernels  80.8 us (98%)
  local copies, waits for them, and re-layouts  1.89 us (2%)
    pallas_call x1, Pallas kernels, on_device(): pl.pallas_call(functools.partial(kernel, scale), out_shape=jax.ShapeDtype...  80.8 us
    unnamed x1, local copies, waits for them, and re-layouts  1.89 us

profile of v2, /device:TPU:1, one launch (start us, length us, event | category | flops | bytes accessed | tf_op | source)
XLA Modules:
  0.0 82.6 jit_solution(261814942342782208)
XLA Ops:
  0.0 80.8 %focus_gram.1 = f32[2,64,1024]{2,1,0:T(8,128)} custom-call(bf16[3,2,64,4096]{3,2,1,0:T(8,128)(2,1)} %foc.1, bf16[3,2,64,128]{3,2,1,0:T(8,128)(2,1)} %snap_hbm.1), custom_call_target="tpu_custom_call" | custom-call | tf_op jit(solution)/shard_map/focus_gram/pallas_call | solution.py:300
  80.8 1.9 %copy.4 = f32[2,64,1024]{2,1,0:T(8,128)} copy(f32[2,64,1024]{2,1,0:T(8,128)} %focus_gram.1) | data formatting | bytes 1048576

commit v3 on v2

--- a/solution.py
+++ b/solution.py
@@ -16,14 +16,15 @@
     (1, "X", 0, 32), (1, "Y", 32, 32),
     (2, "Z", 0, 64),
 )
-ORDER = (0, 1, 2)
+ORDER = (2, 0, 1)
 WHEN = {
     "X": {0: (0.2, 5, 12), 1: (0.4, 9, 18)},
     "Y": {0: (0.1, 4.5, 9, 16, 20), 1: (0.3, 8.5, 12, 19, 25)},
     "Z": {2: (0, 3, 6, 11, 16, 21)},
 }
-DONE = {0: 30, 1: 36, 2: 40}
-GRAM = {0: 41, 1: 42, 2: 50}
+DONE = {2: 26, 0: 30, 1: 40}
+ROWS = {2: 41, 0: 42, 1: 44}
+GRAM = {2: 45.5, 0: 45.7, 1: 50}
 N_COPIES = 256
 
 
@@ -31,7 +32,7 @@
     return lax.dot_general(left, right, (((1,), (1,)), ((), ())), preferred_element_type=F32)
 
 
-def kernel(scale, foc, snap_hbm, out, snap, T, X, yrow, ycol, G, gin, S, R, tsem, ssem, rsem):
+def kernel(scale, foc, snap_hbm, out, snap, T, X, yrow, ycol, G, S, R, tsem, ssem, rsem):
     b = lax.axis_index("bin")
     row = lax.axis_index("row")
     xl, c = b // 2, b % 2
@@ -202,7 +203,6 @@
             event(when[2 + far], functools.partial(later, far))
 
     def done(k):
-        w = gathers[k] = []
         wait_all(pending[k])
         loads[k].wait()
 
@@ -216,55 +216,70 @@
         real = acc[:64, :128] - acc[64:, 128:]
         imag = acc[:64, 128:] + acc[64:, :128]
         focused = jnp.concatenate([real, imag], axis=1).astype(BF16)
-        yrow[k, xh, y] = focused
-        ycol[k, z] = focused
-        own = ycol.at[k, z]
-        for d in (4, 3, 5, 2, 6, 1, 7):
-            w.append(send(own, own, ycol.at[k, (z + 8 - d) % 8], at(dz=d)))
-        own = yrow.at[k, xh, y]
-        for dx, dy in ((1, 2), (1, 1), (1, 3), (1, 0), (0, 2), (0, 1), (0, 3)):
-            w.append(send(own, own, yrow.at[k, (xh + dx) % 2, (y + 4 - dy) % 4], at(dx=dx, dy=dy)))
-
-    def gathered(k):
-        wait_all(gathers[k])
-        if k != ORDER[2]:
-            for part in range(2):
-                for half in range(2):
-                    gram(k, part, half)
-
-    gathers = {}
-    def gram(k, part, half):
-        left = yrow[k, half].reshape(256, 256)
-        right = jnp.concatenate(
-            [ycol[k, pl.ds(2 * part, 2)].reshape(128, 256), ycol[k, pl.ds(4 + 2 * part, 2)].reshape(128, 256)], axis=0
+        yrow[k, 0, xh, y] = focused
+        own = yrow.at[k, 0, xh, y]
+        side, slot = (z // 2) % 2, (z // 4) * 2 + z % 2
+        base = count[0]
+        count[0] += 8
+        place, landed = ycol.at[k, c, slot], rsem.at[base + slot * 2 + c]
+        for n, d in enumerate((4, 3, 5, 2, 6, 1, 7)):
+            copy = pltpu.make_async_remote_copy(
+                src_ref=own, dst_ref=place, send_sem=ssem.at[base + n], recv_sem=landed,
+                device_id=(xl * 2 + side, at(dz=d)[1]), device_id_type=MESH,
+            )
+            copy.start()
+            sent.append(copy)
+        copy = pltpu.make_async_remote_copy(
+            src_ref=own, dst_ref=place, send_sem=ssem.at[base + 7], recv_sem=landed,
+            device_id=sibling, device_id_type=MESH,
         )
-        turned = jnp.concatenate([-right[:, 128:], right[:, :128]], axis=1)
-        if k == ORDER[0]:
-            G[part, half, 0] = dot_t(left, right)
-            G[part, half, 1] = dot_t(left, turned)
-        else:
-            G[part, half, 0] += dot_t(left, right)
-            G[part, half, 1] += dot_t(left, turned)
-
-    for k, kind, first_row, rows in PIECES:
+        pl.when(side != c)(copy.start)
+        to_sibling.append((side != c, copy))
+        pl.when(side == c)(pltpu.make_async_copy(own, place, landed).start)
+        columns[k] = [
+            pltpu.make_async_copy(ycol.at[k, s, j], ycol.at[k, s, j], rsem.at[base + j * 2 + s]).wait
+            for j in range(4)
+            for s in range(2)
+        ]
+        own = yrow.at[k, 0, xh, y]
+        rows[k] = [
+            send(own, own, yrow.at[k, 0, (xh + dx) % 2, (y + 4 - dy) % 4], at(dx=dx, dy=dy))
+            for dx, dy in ((1, 2), (1, 1), (1, 3), (1, 0), (0, 2), (0, 1), (0, 3))
+        ]
+
+    def rows_here(k):
+        wait_all(rows[k])
+        shared[k] = [send(yrow.at[k, 0], yrow.at[k, 1], yrow.at[k, 1], sibling)]
+
+    def gram_both(k):
+        wait_all(shared[k])
+        wait_all(columns[k])
+        mine, other = ycol[k, c].reshape(256, 256), ycol[k, 1 - c].reshape(256, 256)
+        right = jnp.concatenate([mine, other], axis=1)
+        turned = jnp.concatenate([-mine[:, 128:], mine[:, :128], -other[:, 128:], other[:, :128]], axis=1)
+        for half in range(2):
+            left = jnp.concatenate([yrow[k, s, half].reshape(256, 256) for s in range(2)], axis=1)
+            if k == ORDER[0]:
+                G[half, 0] = dot_t(left, right)
+                G[half, 1] = dot_t(left, turned)
+            else:
+                G[half, 0] += dot_t(left, right)
+                G[half, 1] += dot_t(left, turned)
+
+    rows, columns, shared, to_sibling = {}, {}, {}, []
+    for k, kind, first_row, n_rows in PIECES:
         make = {"X": order_x, "Y": order_y, "Z": order_z}[kind]
-        make(k, pl.ds(first_row, rows), WHEN[kind][k])
+        make(k, pl.ds(first_row, n_rows), WHEN[kind][k])
     for k in ORDER:
         event(DONE[k], functools.partial(done, k))
-        event(GRAM[k], functools.partial(gathered, k))
+        event(ROWS[k], functools.partial(rows_here, k))
+        event(GRAM[k], functools.partial(gram_both, k))
     for e in sorted(events, key=lambda e: e[:2]):
         e[2]()
 
-    waits = []
-    for half in ((xh + 1) % 2, xh):
-        gram(ORDER[2], 1 - c, half)
-        piece = G.at[1 - c, half]
-        waits.append(send(piece, gin.at[half], gin.at[half], sibling))
     final = []
     for n, half in enumerate(((xh + 1) % 2, xh)):
-        gram(ORDER[2], c, half)
-        waits[n]()
-        total = (G[c, half] + gin[half]) * scale
+        total = G[half] * scale
         for part in range(2):
             S[part, half] = total[:, :, part * 128 : (part + 1) * 128].reshape(2, 4, 64, 128).astype(BF16)
         dx = 1 - n
@@ -293,6 +308,8 @@
                 )
     for copy in sent:
         copy.wait_send()
+    for started, copy in to_sibling:
+        pl.when(started)(copy.wait_send)
 
 
 def on_device(focusing, snapshots):
@@ -306,9 +323,8 @@
             pltpu.VMEM((3, 2, 64, 128), BF16),
             pltpu.VMEM((3, 2, 64, 4096), BF16),
             pltpu.VMEM((3, 8, 2, 4, 64, 256), BF16),
+            pltpu.VMEM((3, 2, 2, 4, 64, 256), BF16),
             pltpu.VMEM((3, 2, 4, 64, 256), BF16),
-            pltpu.VMEM((3, 8, 64, 256), BF16),
-            pltpu.VMEM((2, 2, 2, 256, 256), F32),
             pltpu.VMEM((2, 2, 256, 256), F32),
             pltpu.VMEM((2, 2, 2, 4, 64, 128), BF16),
             pltpu.VMEM((2, 2, 4, 2, 64, 128), BF16),

time: 82.8 us -> 79.7 us (0.963)
  Pallas kernels: 80.8 us -> 77.7 us
    pallas_call x1, Pallas kernels: 80.8 us -> 77.7 us  [on_device(): pl.pallas_call(functools.partial(kernel, scale), out_shape=jax.ShapeDtype...]
where the time goes in v3:
time: 79.7 us; the launch traced here: 79.6 us
  Pallas kernels  77.7 us (97%)
  local copies, waits for them, and re-layouts  1.89 us (2%)
    pallas_call x1, Pallas kernels, on_device(): pl.pallas_call(functools.partial(kernel, scale), out_shape=jax.ShapeDtype...  77.7 us
    unnamed x1, local copies, waits for them, and re-layouts  1.89 us

profile of v3, /device:TPU:1, one launch (start us, length us, event | category | flops | bytes accessed | tf_op | source)
XLA Modules:
  0.0 79.6 jit_solution(15116201953455375546)
XLA Ops:
  0.0 77.7 %focus_gram.1 = f32[2,64,1024]{2,1,0:T(8,128)} custom-call(bf16[3,2,64,4096]{3,2,1,0:T(8,128)(2,1)} %foc.1, bf16[3,2,64,128]{3,2,1,0:T(8,128)(2,1)} %snap_hbm.1), custom_call_target="tpu_custom_call" | custom-call | tf_op jit(solution)/shard_map/focus_gram/pallas_call | solution.py:317
  77.7 1.9 %copy.4 = f32[2,64,1024]{2,1,0:T(8,128)} copy(f32[2,64,1024]{2,1,0:T(8,128)} %focus_gram.1) | data formatting | bytes 1048576

commit v4 on v2

--- a/solution.py
+++ b/solution.py
@@ -11,40 +11,41 @@
 BF16 = jnp.bfloat16
 F32 = jnp.float32
 
-PIECES = (
-    (0, "X", 0, 32), (0, "Y", 32, 32),
-    (1, "X", 0, 32), (1, "Y", 32, 32),
-    (2, "Z", 0, 64),
-)
-ORDER = (0, 1, 2)
-WHEN = {
-    "X": {0: (0.2, 5, 12), 1: (0.4, 9, 18)},
-    "Y": {0: (0.1, 4.5, 9, 16, 20), 1: (0.3, 8.5, 12, 19, 25)},
-    "Z": {2: (0, 3, 6, 11, 16, 21)},
-}
-DONE = {0: 30, 1: 36, 2: 40}
-GRAM = {0: 41, 1: 42, 2: 50}
-N_COPIES = 256
+PIECES = (("Z", 0, 64),)
+WHEN = {"X": (0.5, 8, 15), "Z": (0, 3, 6, 11, 16, 21)}
+SHARED = ((0, 32), (32, 32))
+SHARED_WHEN = ((0.1, 3.1, 5, 0.5, 12, 9), (0.2, 3.2, 6.8, 0.5, 13, 9.5))
+SWAP_WHEN = (3.3, 3.4, 6.1, 6.2)
+DONE_2, ROWS_2, GRAM_2 = 36, 44, 50
+DONE_M, ROWS_M, GRAM_M = 30, 40, 45
+N_COPIES = 288
+NEAR_FIRST = (1, 7, 2, 6, 3, 5, 4)
 
 
 def dot_t(left, right):
     return lax.dot_general(left, right, (((1,), (1,)), ((), ())), preferred_element_type=F32)
 
 
-def kernel(scale, foc, snap_hbm, out, snap, T, X, yrow, ycol, G, gin, S, R, tsem, ssem, rsem):
+def kernel(scale, foc, snap_hbm, out, snap, T, given, X, yrow, ycol, G, S, R, tsem, ssem, rsem):
     b = lax.axis_index("bin")
     row = lax.axis_index("row")
     xl, c = b // 2, b % 2
     z, xh, y = row // 8, (row // 4) % 2, row % 4
+    mine = 1 - ((y + 1) // 2) % 2
+    first_y = (y // 2) * 2
+    swap_y = first_y * 2 + 1 - y
 
     def at(dz=0, dx=0, dy=0):
         return (b, ((z + dz) % 8) * 8 + ((xh + dx) % 2) * 4 + (y + dy) % 4)
 
     fetch = pltpu.make_async_copy(snap_hbm, snap, tsem.at[3])
     fetch.start()
-    loads = [pltpu.make_async_copy(foc.at[k], T.at[k], tsem.at[k]) for k in range(3)]
-    for k in range(3):
-        loads[k].start()
+    loads = [
+        pltpu.make_async_copy(foc.at[mine], T.at[0], tsem.at[0]),
+        pltpu.make_async_copy(foc.at[2], T.at[2], tsem.at[2]),
+    ]
+    for load in loads:
+        load.start()
 
     partners = [at(dz=d) for d in range(1, 8)]
     for dl in range(2):
@@ -59,8 +60,9 @@
         pl.semaphore_signal(barrier, inc=1, device_id=peer, device_id_type=MESH)
 
     fetch.wait()
-    for k in range(3):
-        X[k, z, xh, y] = jnp.concatenate([snap[k, 0], snap[k, 1]], axis=1)
+    X[0, z, xh, y] = jnp.concatenate([snap[mine, 0], snap[mine, 1]], axis=1)
+    X[2, z, xh, y] = jnp.concatenate([snap[2, 0], snap[2, 1]], axis=1)
+    given[...] = jnp.concatenate([snap[1 - mine, 0], snap[1 - mine, 1]], axis=1)
 
     pl.semaphore_wait(barrier, len(partners))
 
@@ -85,7 +87,7 @@
             w()
 
     events = []
-    pending = {k: [] for k in range(3)}
+    pending = {0: [], 2: []}
 
     def event(when, step):
         events.append((when, len(events), step))
@@ -118,43 +120,80 @@
         for t, step in zip(when, (first, second, third)):
             event(t, step)
 
-    def order_y(k, rs, when):
+    def shared_bin(rs, when, x_first):
         w = {}
-        low, high = pl.ds(0, 4), pl.ds(4, 4)
-
-        def to_y(h):
-            own = X.at[k, :, h, y, rs]
-            return [send(own, own, X.at[k, :, h, (y + 4 - d) % 4, rs], at(dy=d)) for d in (1, 3)]
-
-        def on_y(h, arrivals):
-            arrivals[0]()
-            piece = X.at[k, low, h, (y + 3) % 4, rs]
-            pending[k].append(send(piece, piece, X.at[k, low, h, (y + 2) % 4, rs], at(dy=1)))
-            arrivals[1]()
-            piece = X.at[k, high, h, (y + 1) % 4, rs]
-            pending[k].append(send(piece, piece, X.at[k, high, h, (y + 2) % 4, rs], at(dy=3)))
+        swapper = (b, z * 8 + xh * 4 + swap_y)
+        facing = (b, z * 8 + xh * 4 + 3 - y)
+        both, far = pl.ds(first_y, 2), pl.ds(2 - first_y, 2)
+
+        def over_z(line):
+            own = X.at[0, z, xh, line, rs]
+            return {d: send(own, own, X.at[0, (z + 8 - d) % 8, xh, line, rs], at(dz=d)) for d in (2, 6, 1, 7)}
+
+        w["x"], w["facing"] = [], []
+
+        def spread(d):
+            own = X.at[0, (z + 8 - d) % 8, xh, both, rs]
+            w["x"].append(send(own, own, X.at[0, (z + 8 - d) % 8, 1 - xh, both, rs], at(dx=1)))
+            w["facing"].append(send(own, own, X.at[0, (z + 8 - d) % 8, xh, far, rs], facing))
 
         def first():
-            w["z"] = z_direct(k, rs)
+            w["pair"] = send(given.at[rs], X.at[0, z, xh, y, rs], X.at[0, z, xh, swap_y, rs], swapper)
+            w["own"] = over_z(y)
 
         def second():
-            wait_all(w["z"])
-            own = X.at[k, :, xh, y, rs]
-            w["x"] = send(own, own, X.at[k, :, 1 - xh, y, rs], at(dx=1))
-            w["a"] = to_y(xh)
-
-        def third():
-            w["x"]()
-            w["b"] = to_y(1 - xh)
+            w["pair"]()
+            w["other"] = over_z(swap_y)
+            spread(0)
+
+        def pass_on(d, onward, part):
+            block = X.at[0, (z + 8 - d) % 8, xh, both, rs]
+            w[3 if onward == 1 else 5] = send(
+                block, block, X.at[0, (z + 8 - onward - d) % 8, xh, both, rs], at(dz=onward)
+            )
+            block = X.at[0, (z + 8 - d) % 8, xh, both, part]
+            w.setdefault(4, []).append(send(block, block, X.at[0, (z + 4) % 8, xh, both, part], at(dz=d)))
+
+        def third(d):
+            w["own"][d]()
+            w["other"][d]()
+            if d == 2:
+                pass_on(2, 1, pl.ds(rs.start, rs.size // 2))
+            if d == 6:
+                pass_on(6, 7, pl.ds(rs.start + rs.size // 2, rs.size // 2))
+            spread(d)
+
+        def relayed():
+            for d in (3, 5):
+                w[d]()
+                spread(d)
+            wait_all(w[4])
+            spread(4)
 
         def fourth():
-            on_y(xh, w["a"])
-
-        def fifth():
-            on_y(1 - xh, w["b"])
-
-        for t, step in zip(when, (first, second, third, fourth, fifth)):
-            event(t, step)
+            if x_first:
+                wait_all(w["x"])
+                own = X.at[0, :, 1 - xh, both, rs]
+                pending[0].append(send(own, own, X.at[0, :, 1 - xh, far, rs], facing))
+                pending[0].extend(w["facing"])
+            else:
+                wait_all(w["facing"])
+                own = X.at[0, :, xh, far, rs]
+                pending[0].append(send(own, own, X.at[0, :, 1 - xh, far, rs], at(dx=1)))
+                pending[0].extend(w["x"])
+
+        event(when[0], first)
+        event(when[1], second)
+        for n, d in enumerate((2, 6, 1, 7)):
+            event(when[2] + n * when[3], functools.partial(third, d))
+        event(when[5], relayed)
+        event(when[4], fourth)
+
+    def swap(n):
+        quarter = pl.ds(n * 1024, 1024)
+        there = T.at[1, :, :, quarter]
+        swapper = (b, z * 8 + xh * 4 + swap_y)
+        pending[0].append(send(foc.at[1 - mine, :, :, quarter], there, there, swapper))
 
     def order_z(k, rs, when):
         w = {}
@@ -201,70 +240,136 @@
         for far in range(1, 4):
             event(when[2 + far], functools.partial(later, far))
 
-    def done(k):
-        w = gathers[k] = []
-        wait_all(pending[k])
-        loads[k].wait()
+    side, slot = (z // 2) % 2, (z // 4) * 2 + z % 2
+
+    def give_columns(k, own, line, local):
+        base = count[0]
+        count[0] += 16
+        place, landed = ycol.at[k, c, slot], rsem.at[base + slot * 2 + c]
+        for n, d in enumerate((4, 3, 5, 2, 6, 1, 7) if local else (4, 3, 5, 2, 6, 1, 7, 0)):
+            to = ((z + d) % 8) * 8 + xh * 4 + line
+            copy = pltpu.make_async_remote_copy(
+                src_ref=own, dst_ref=place, send_sem=ssem.at[base + n], recv_sem=landed,
+                device_id=(xl * 2 + side, to), device_id_type=MESH,
+            )
+            copy.start()
+            sent.append(copy)
+        if local:
+            copy = pltpu.make_async_remote_copy(
+                src_ref=own, dst_ref=place, send_sem=ssem.at[base + 8], recv_sem=landed,
+                device_id=sibling, device_id_type=MESH,
+            )
+            pl.when(side != c)(copy.start)
+            to_sibling.append((side != c, copy))
+            pl.when(side == c)(pltpu.make_async_copy(own, place, landed).start)
+        return base
+
+    def take_columns(k, base):
+        return [
+            pltpu.make_async_copy(ycol.at[k, s, j], ycol.at[k, s, j], rsem.at[base + j * 2 + s]).wait
+            for j in range(4)
+            for s in range(2)
+        ]
+
+    def complex_parts(acc):
+        real = acc[:64, :128] - acc[64:, 128:]
+        imag = acc[:64, 128:] + acc[64:, :128]
+        return jnp.concatenate([real, imag], axis=1).astype(BF16)
+
+    others = ((1, 2), (1, 1), (1, 3), (1, 0), (0, 2), (0, 1), (0, 3))
+
+    def done_2():
+        wait_all(pending[2])
+        loads[1].wait()
 
         def plane(i, acc):
             cols = pl.ds(pl.multiple_of(i * 512, 512), 512)
             return acc + jnp.dot(
-                T[k, :, :, cols].reshape(128, 512), X[k, i].reshape(512, 256), preferred_element_type=F32
+                T[2, :, :, cols].reshape(128, 512), X[2, i].reshape(512, 256), preferred_element_type=F32
             )
 
-        acc = lax.fori_loop(0, 8, plane, jnp.zeros((128, 256), F32))
-        real = acc[:64, :128] - acc[64:, 128:]
-        imag = acc[:64, 128:] + acc[64:, :128]
-        focused = jnp.concatenate([real, imag], axis=1).astype(BF16)
-        yrow[k, xh, y] = focused
-        ycol[k, z] = focused
-        own = ycol.at[k, z]
-        for d in (4, 3, 5, 2, 6, 1, 7):
-            w.append(send(own, own, ycol.at[k, (z + 8 - d) % 8], at(dz=d)))
-        own = yrow.at[k, xh, y]
-        for dx, dy in ((1, 2), (1, 1), (1, 3), (1, 0), (0, 2), (0, 1), (0, 3)):
-            w.append(send(own, own, yrow.at[k, (xh + dx) % 2, (y + 4 - dy) % 4], at(dx=dx, dy=dy)))
-
-    def gathered(k):
-        wait_all(gathers[k])
-        if k != ORDER[2]:
+        yrow[2, 0, xh, y] = complex_parts(lax.fori_loop(0, 8, plane, jnp.zeros((128, 256), F32)))
+        own = yrow.at[2, 0, xh, y]
+        columns[2] = take_columns(2, give_columns(2, own, y, True))
+        rows[2] = [
+            send(own, own, yrow.at[2, 0, (xh + dx) % 2, (y + 4 - dy) % 4], at(dx=dx, dy=dy)) for dx, dy in others
+        ]
+
+    def done_mine():
+        loads[0].wait()
+        wait_all(pending[0])
+
+        def plane(i, acc):
+            cols = pl.ds(pl.multiple_of(i * 512, 512), 512)
+            return acc + jnp.dot(
+                T[pl.ds(0, 2), :, :, cols].reshape(256, 512), X[0, i].reshape(512, 256), preferred_element_type=F32
+            )
+
+        acc = lax.fori_loop(0, 8, plane, jnp.zeros((256, 256), F32))
+        yrow[mine, 0, xh, y] = complex_parts(acc[:128])
+        yrow[mine, 0, xh, swap_y] = complex_parts(acc[128:])
+        first_base = give_columns(mine, yrow.at[mine, 0, xh, y], y, True)
+        second_base = give_columns(mine, yrow.at[mine, 0, xh, swap_y], swap_y, False)
+        columns[0] = take_columns(mine, first_base) + take_columns(1 - mine, second_base)
+        both = yrow.at[mine, 0, xh, pl.ds(first_y, 2)]
+        rows[0] = []
+        for dx, dy in others:
+            from_y = (y + 4 - dy) % 4
+            landing = yrow.at[1 - ((from_y + 1) // 2) % 2, 0, (xh + dx) % 2, pl.ds((from_y // 2) * 2, 2)]
+            rows[0].append(send(both, both, landing, at(dx=dx, dy=dy)))
+
+    def rows_here(k):
+        wait_all(rows[k])
+        shared[k] = [
+            send(yrow.at[i, 0], yrow.at[i, 1], yrow.at[i, 1], sibling) for i in ((0, 1) if k == 0 else (2,))
+        ]
+
+    def operands(k):
+        one, two = ycol[k, c].reshape(256, 256), ycol[k, 1 - c].reshape(256, 256)
+        right = jnp.concatenate([one, two], axis=1)
+        return right, jnp.concatenate([-one[:, 128:], one[:, :128], -two[:, 128:], two[:, :128]], axis=1)
+
+    def half_tile(k, half, pair):
+        left = jnp.concatenate([yrow[k, s, half].reshape(256, 256) for s in range(2)], axis=1)
+        return [dot_t(left, side_by) for side_by in pair]
+
+    def gram_mine():
+        wait_all(shared[0])
+        wait_all(columns[0])
+        pairs = operands(0), operands(1)
+        for half in range(2):
+            tiles = half_tile(0, half, pairs[0]), half_tile(1, half, pairs[1])
             for part in range(2):
-                for half in range(2):
-                    gram(k, part, half)
-
-    gathers = {}
-    def gram(k, part, half):
-        left = yrow[k, half].reshape(256, 256)
-        right = jnp.concatenate(
-            [ycol[k, pl.ds(2 * part, 2)].reshape(128, 256), ycol[k, pl.ds(4 + 2 * part, 2)].reshape(128, 256)], axis=0
-        )
-        turned = jnp.concatenate([-right[:, 128:], right[:, :128]], axis=1)
-        if k == ORDER[0]:
-            G[part, half, 0] = dot_t(left, right)
-            G[part, half, 1] = dot_t(left, turned)
-        else:
-            G[part, half, 0] += dot_t(left, right)
-            G[part, half, 1] += dot_t(left, turned)
-
-    for k, kind, first_row, rows in PIECES:
-        make = {"X": order_x, "Y": order_y, "Z": order_z}[kind]
-        make(k, pl.ds(first_row, rows), WHEN[kind][k])
-    for k in ORDER:
-        event(DONE[k], functools.partial(done, k))
-        event(GRAM[k], functools.partial(gathered, k))
+                G[half, part] = tiles[0][part] + tiles[1][part]
+
+    def gram_2():
+        wait_all(shared[2])
+        wait_all(columns[2])
+        last.extend(operands(2))
+
+    rows, columns, shared, to_sibling, last = {}, {}, {}, [], []
+    for kind, first_row, n_rows in PIECES:
+        make = {"X": order_x, "Z": order_z}[kind]
+        make(2, pl.ds(first_row, n_rows), WHEN[kind])
+    for (first_row, n_rows), when in zip(SHARED, SHARED_WHEN):
+        shared_bin(pl.ds(first_row, n_rows), when, first_row == 0)
+    for n in range(4):
+        event(SWAP_WHEN[n], functools.partial(swap, n))
+    event(DONE_2, done_2)
+    event(ROWS_2, functools.partial(rows_here, 2))
+    event(GRAM_2, gram_2)
+    event(DONE_M, done_mine)
+    event(ROWS_M, functools.partial(rows_here, 0))
+    event(GRAM_M, gram_mine)
     for e in sorted(events, key=lambda e: e[:2]):
         e[2]()
 
-    waits = []
-    for half in ((xh + 1) % 2, xh):
-        gram(ORDER[2], 1 - c, half)
-        piece = G.at[1 - c, half]
-        waits.append(send(piece, gin.at[half], gin.at[half], sibling))
     final = []
+    before_final = len(sent)
     for n, half in enumerate(((xh + 1) % 2, xh)):
-        gram(ORDER[2], c, half)
-        waits[n]()
-        total = (G[c, half] + gin[half]) * scale
+        for part, term in enumerate(half_tile(2, half, last)):
+            G[half, part] += term
+        total = G[half] * scale
         for part in range(2):
             S[part, half] = total[:, :, part * 128 : (part + 1) * 128].reshape(2, 4, 64, 128).astype(BF16)
         dx = 1 - n
@@ -280,6 +385,10 @@
                     )
                 )
     R[xl, xh, y] = S[xl, xh, :, y]
+    for copy in sent[:before_final]:
+        copy.wait_send()
+    for started, copy in to_sibling:
+        pl.when(started)(copy.wait_send)
     wait_all(final)
     for zi in range(2):
         for h in range(2):
@@ -291,7 +400,7 @@
                 out[:, :, zi * 512 + h * 256 + yp * 128 : zi * 512 + h * 256 + yp * 128 + 128] = jnp.concatenate(
                     [pair[0][:, :, lanes], pair[1][:, :, lanes]], axis=2
                 )
-    for copy in sent:
+    for copy in sent[before_final:]:
         copy.wait_send()
 
 
@@ -305,10 +414,10 @@
         scratch_shapes=[
             pltpu.VMEM((3, 2, 64, 128), BF16),
             pltpu.VMEM((3, 2, 64, 4096), BF16),
+            pltpu.VMEM((64, 256), BF16),
             pltpu.VMEM((3, 8, 2, 4, 64, 256), BF16),
+            pltpu.VMEM((3, 2, 2, 4, 64, 256), BF16),
             pltpu.VMEM((3, 2, 4, 64, 256), BF16),
-            pltpu.VMEM((3, 8, 64, 256), BF16),
-            pltpu.VMEM((2, 2, 2, 256, 256), F32),
             pltpu.VMEM((2, 2, 256, 256), F32),
             pltpu.VMEM((2, 2, 2, 4, 64, 128), BF16),
             pltpu.VMEM((2, 2, 4, 2, 64, 128), BF16),

time: 82.8 us -> 76.1 us (0.919)
  Pallas kernels: 80.8 us -> 74.1 us
    pallas_call x1, Pallas kernels: 80.8 us -> 74.1 us  [on_device(): pl.pallas_call(functools.partial(kernel, scale), out_shape=jax.ShapeDtype...]
where the time goes in v4:
time: 76.1 us; the launch traced here: 76 us
  Pallas kernels  74.1 us (97%)
  local copies, waits for them, and re-layouts  1.89 us (2%)
    pallas_call x1, Pallas kernels, on_device(): pl.pallas_call(functools.partial(kernel, scale), out_shape=jax.ShapeDtype...  74.1 us
    unnamed x1, local copies, waits for them, and re-layouts  1.89 us

profile of v4, /device:TPU:1, one launch (start us, length us, event | category | flops | bytes accessed | tf_op | source)
XLA Modules:
  0.0 76.0 jit_solution(9615090199869075674)
XLA Ops:
  0.0 74.1 %focus_gram.1 = f32[2,64,1024]{2,1,0:T(8,128)} custom-call(bf16[3,2,64,4096]{3,2,1,0:T(8,128)(2,1)} %foc.1, bf16[3,2,64,128]{3,2,1,0:T(8,128)(2,1)} %snap_hbm.1), custom_call_target="tpu_custom_call" | custom-call | tf_op jit(solution)/shard_map/focus_gram/pallas_call | solution.py:409
  74.1 1.9 %copy.4 = f32[2,64,1024]{2,1,0:T(8,128)} copy(f32[2,64,1024]{2,1,0:T(8,128)} %focus_gram.1) | data formatting | bytes 1048576

commit v5 on v4

--- a/solution.py
+++ b/solution.py
@@ -18,7 +18,9 @@
 SWAP_WHEN = (3.3, 3.4, 6.1, 6.2)
 DONE_2, ROWS_2, GRAM_2 = 36, 44, 50
 DONE_M, ROWS_M, GRAM_M = 30, 40, 45
-N_COPIES = 288
+TWO_STEPS = (2,)
+RELAY_M, RELAY_2 = 36.5, 43
+N_COPIES = 320
 NEAR_FIRST = (1, 7, 2, 6, 3, 5, 4)
 
 
@@ -246,7 +248,8 @@
         base = count[0]
         count[0] += 16
         place, landed = ycol.at[k, c, slot], rsem.at[base + slot * 2 + c]
-        for n, d in enumerate((4, 3, 5, 2, 6, 1, 7) if local else (4, 3, 5, 2, 6, 1, 7, 0)):
+        direct = (2, 6, 1, 7) if k is mine or k in TWO_STEPS else (4, 3, 5, 2, 6, 1, 7)
+        for n, d in enumerate(direct if local else direct + (0,)):
             to = ((z + d) % 8) * 8 + xh * 4 + line
             copy = pltpu.make_async_remote_copy(
                 src_ref=own, dst_ref=place, send_sem=ssem.at[base + n], recv_sem=landed,
@@ -256,7 +259,7 @@
             sent.append(copy)
         if local:
             copy = pltpu.make_async_remote_copy(
-                src_ref=own, dst_ref=place, send_sem=ssem.at[base + 8], recv_sem=landed,
+                src_ref=own, dst_ref=place, send_sem=ssem.at[base + 7], recv_sem=landed,
                 device_id=sibling, device_id_type=MESH,
             )
             pl.when(side != c)(copy.start)
@@ -264,12 +267,62 @@
             pl.when(side == c)(pltpu.make_async_copy(own, place, landed).start)
         return base
 
-    def take_columns(k, base):
-        return [
-            pltpu.make_async_copy(ycol.at[k, s, j], ycol.at[k, s, j], rsem.at[base + j * 2 + s]).wait
-            for j in range(4)
-            for s in range(2)
-        ]
+    near = ((((z + 6) % 8) // 4) * 2 + z % 2, (((z + 2) % 8) // 4) * 2 + z % 2)
+    rest = tuple(j + 1 - 2 * (j % 2) for j in near)
+
+    def column_wait(k, base, j, s):
+        return pltpu.make_async_copy(ycol.at[k, s, j], ycol.at[k, s, j], rsem.at[base + j * 2 + s]).wait
+
+    def relay_columns(k, base):
+        copies = []
+        for s in range(2):
+            for up, j in enumerate(near):
+                for hop, part in ((1, pl.ds(0, 64)), (2, pl.ds(32 * up, 32))):
+                    block = ycol.at[k, s, j, part]
+                    to = ((z + 8 + (hop - 2 * hop * up)) % 8) * 8 + xh * 4 + y
+                    copies.append(
+                        pltpu.make_async_remote_copy(
+                            src_ref=block, dst_ref=block, send_sem=ssem.at[base + 8 + len(copies)],
+                            recv_sem=rsem.at[base + j * 2 + s], device_id=(b, to), device_id_type=MESH,
+                        )
+                    )
+
+        def relay():
+            for s in range(2):
+                for up, j in enumerate(near):
+                    column_wait(k, base, j, s)()
+                    for copy in copies[4 * s + 2 * up : 4 * s + 2 * up + 2]:
+                        copy.start()
+
+        pl.when(side != c)(relay)
+        to_sibling.extend((side != c, copy) for copy in copies)
+
+    def take_columns(k, base, relayed):
+        def take():
+            for s in range(2):
+                for j in rest:
+                    column_wait(k, base, j, s)()
+
+            def take_near():
+                for s in range(2):
+                    for j in near:
+                        column_wait(k, base, j, s)()
+
+            if relayed:
+                pl.when(side == c)(take_near)
+            else:
+                take_near()
+
+        return [take]
+
+    def relay_2():
+        relay_columns(2, bases[2])
+
+    def relay_mine():
+        relay_columns(mine, bases[0])
+        relay_columns(1 - mine, bases[1])
+
+    bases = {}
 
     def complex_parts(acc):
         real = acc[:64, :128] - acc[64:, 128:]
@@ -290,7 +343,8 @@
 
         yrow[2, 0, xh, y] = complex_parts(lax.fori_loop(0, 8, plane, jnp.zeros((128, 256), F32)))
         own = yrow.at[2, 0, xh, y]
-        columns[2] = take_columns(2, give_columns(2, own, y, True))
+        bases[2] = give_columns(2, own, y, True)
+        columns[2] = take_columns(2, bases[2], 2 in TWO_STEPS)
         rows[2] = [
             send(own, own, yrow.at[2, 0, (xh + dx) % 2, (y + 4 - dy) % 4], at(dx=dx, dy=dy)) for dx, dy in others
         ]
@@ -308,9 +362,9 @@
         acc = lax.fori_loop(0, 8, plane, jnp.zeros((256, 256), F32))
         yrow[mine, 0, xh, y] = complex_parts(acc[:128])
         yrow[mine, 0, xh, swap_y] = complex_parts(acc[128:])
-        first_base = give_columns(mine, yrow.at[mine, 0, xh, y], y, True)
-        second_base = give_columns(mine, yrow.at[mine, 0, xh, swap_y], swap_y, False)
-        columns[0] = take_columns(mine, first_base) + take_columns(1 - mine, second_base)
+        bases[0] = give_columns(mine, yrow.at[mine, 0, xh, y], y, True)
+        bases[1] = give_columns(mine, yrow.at[mine, 0, xh, swap_y], swap_y, False)
+        columns[0] = take_columns(mine, bases[0], True) + take_columns(1 - mine, bases[1], True)
         both = yrow.at[mine, 0, xh, pl.ds(first_y, 2)]
         rows[0] = []
         for dx, dy in others:
@@ -356,6 +410,9 @@
     for n in range(4):
         event(SWAP_WHEN[n], functools.partial(swap, n))
     event(DONE_2, done_2)
+    event(RELAY_M, relay_mine)
+    if 2 in TWO_STEPS:
+        event(RELAY_2, relay_2)
     event(ROWS_2, functools.partial(rows_here, 2))
     event(GRAM_2, gram_2)
     event(DONE_M, done_mine)

time: 76.1 us -> 72.2 us (0.949)
  the two profiles are of different devices: /device:TPU:1 before, /device:TPU:8 now
where the time goes in v5:
time: 72.2 us; the launch traced here: 72.1 us
  Pallas kernels  70.2 us (97%)
  local copies, waits for them, and re-layouts  1.89 us (3%)
    pallas_call x1, Pallas kernels, on_device(): pl.pallas_call(functools.partial(kernel, scale), out_shape=jax.ShapeDtype...  70.2 us
    unnamed x1, local copies, waits for them, and re-layouts  1.89 us

profile of v5, /device:TPU:8, one launch (start us, length us, event | category | flops | bytes accessed | tf_op | source)
XLA Modules:
  0.0 72.1 jit_solution(11687514186267513195)
XLA Ops:
  0.0 70.2 %focus_gram.1 = f32[2,64,1024]{2,1,0:T(8,128)} custom-call(bf16[3,2,64,4096]{3,2,1,0:T(8,128)(2,1)} %foc.1, bf16[3,2,64,128]{3,2,1,0:T(8,128)(2,1)} %snap_hbm.1), custom_call_target="tpu_custom_call" | custom-call | tf_op jit(solution)/shard_map/focus_gram/pallas_call | solution.py:466
  70.2 1.9 %copy.4 = f32[2,64,1024]{2,1,0:T(8,128)} copy(f32[2,64,1024]{2,1,0:T(8,128)} %focus_gram.1) | data formatting | bytes 1048576

commit v6 on v5

--- a/solution.py
+++ b/solution.py
@@ -49,7 +49,7 @@
     for load in loads:
         load.start()
 
-    partners = [at(dz=d) for d in range(1, 8)]
+    partners = [at(dz=d) for d in (1, 2, 6, 7)]
     for dl in range(2):
         for dx in range(2):
             for dy in range(4):

time: 72.2 us -> 71.9 us (level)
  the two profiles are of different devices: /device:TPU:8 before, /device:TPU:2 now
where the time goes in v6:
time: 71.9 us; the launch traced here: 71.8 us
  Pallas kernels  69.9 us (97%)
  local copies, waits for them, and re-layouts  1.89 us (3%)
    pallas_call x1, Pallas kernels, on_device(): pl.pallas_call(functools.partial(kernel, scale), out_shape=jax.ShapeDtype...  69.9 us
    unnamed x1, local copies, waits for them, and re-layouts  1.89 us

profile of v6, /device:TPU:2, one launch (start us, length us, event | category | flops | bytes accessed | tf_op | source)
XLA Modules:
  0.0 71.8 jit_solution(14468051350867935941)
XLA Ops:
  0.0 69.9 %focus_gram.1 = f32[2,64,1024]{2,1,0:T(8,128)} custom-call(bf16[3,2,64,4096]{3,2,1,0:T(8,128)(2,1)} %foc.1, bf16[3,2,64,128]{3,2,1,0:T(8,128)(2,1)} %snap_hbm.1), custom_call_target="tpu_custom_call" | custom-call | tf_op jit(solution)/shard_map/focus_gram/pallas_call | solution.py:466
  69.9 1.9 %copy.4 = f32[2,64,1024]{2,1,0:T(8,128)} copy(f32[2,64,1024]{2,1,0:T(8,128)} %focus_gram.1) | data formatting | bytes 1048576

commit v7 on v6

--- a/solution.py
+++ b/solution.py
@@ -353,17 +353,19 @@
         loads[0].wait()
         wait_all(pending[0])
 
-        def plane(i, acc):
-            cols = pl.ds(pl.multiple_of(i * 512, 512), 512)
-            return acc + jnp.dot(
-                T[pl.ds(0, 2), :, :, cols].reshape(256, 512), X[0, i].reshape(512, 256), preferred_element_type=F32
-            )
-
-        acc = lax.fori_loop(0, 8, plane, jnp.zeros((256, 256), F32))
-        yrow[mine, 0, xh, y] = complex_parts(acc[:128])
-        yrow[mine, 0, xh, swap_y] = complex_parts(acc[128:])
+        def product(owner):
+            def plane(i, acc):
+                cols = pl.ds(pl.multiple_of(i * 512, 512), 512)
+                return acc + jnp.dot(
+                    T[owner, :, :, cols].reshape(128, 512), X[0, i].reshape(512, 256), preferred_element_type=F32
+                )
+
+            return complex_parts(lax.fori_loop(0, 8, plane, jnp.zeros((128, 256), F32)))
+
+        yrow[mine, 0, xh, swap_y] = product(1)
+        bases[1] = give_columns(mine, yrow.at[mine, 0, xh, swap_y], swap_y, False)
+        yrow[mine, 0, xh, y] = product(0)
         bases[0] = give_columns(mine, yrow.at[mine, 0, xh, y], y, True)
-        bases[1] = give_columns(mine, yrow.at[mine, 0, xh, swap_y], swap_y, False)
         columns[0] = take_columns(mine, bases[0], True) + take_columns(1 - mine, bases[1], True)
         both = yrow.at[mine, 0, xh, pl.ds(first_y, 2)]
         rows[0] = []

time: 71.9 us -> 71.6 us (level)
  the two profiles are of different devices: /device:TPU:2 before, /device:TPU:8 now
where the time goes in v7:
time: 71.6 us; the launch traced here: 71.5 us
  Pallas kernels  69.6 us (97%)
  local copies, waits for them, and re-layouts  1.89 us (3%)
    pallas_call x1, Pallas kernels, on_device(): pl.pallas_call(functools.partial(kernel, scale), out_shape=jax.ShapeDtype...  69.6 us
    unnamed x1, local copies, waits for them, and re-layouts  1.89 us

profile of v7, /device:TPU:8, one launch (start us, length us, event | category | flops | bytes accessed | tf_op | source)
XLA Modules:
  0.0 71.5 jit_solution(173529171508867040)
XLA Ops:
  0.0 69.6 %focus_gram.1 = f32[2,64,1024]{2,1,0:T(8,128)} custom-call(bf16[3,2,64,4096]{3,2,1,0:T(8,128)(2,1)} %foc.1, bf16[3,2,64,128]{3,2,1,0:T(8,128)(2,1)} %snap_hbm.1), custom_call_target="tpu_custom_call" | custom-call | tf_op jit(solution)/shard_map/focus_gram/pallas_call | solution.py:468
  69.6 1.9 %copy.4 = f32[2,64,1024]{2,1,0:T(8,128)} copy(f32[2,64,1024]{2,1,0:T(8,128)} %focus_gram.1) | data formatting | bytes 1048576
